TPU v7x, 512 devices: a whole 4x8x8 slice. The times are simulated.
512 devices in a mesh: section: 64 (over z, y_hi, core), expert: 8 (over x, y_lo).
Axes of the slice: x: 4, y: 8 (y_hi: 4, y_lo: 2; y = y_hi * 2 + y_lo), z: 8, core: 2. Of those that a mesh axis runs over, the one named last changes fastest.
Arguments:
- grad_out: bfloat16 [64, 1024, 4096], P('section', 'expert'), may hold values from -6 to 6
- expert_outputs: bfloat16 [64, 2560, 4096], P('section', 'expert'), may hold values from -0.29882812 to 0.29882812
- expert_ids: int32 [64, 1024, 2], P('section', 'expert'), may hold values from 0 to 7, as said below
- bin_slots: int32 [64, 1024, 2], P('section', 'expert'), may hold values from 0 to 39, as said below
- keep_mask: int32 [64, 1024, 2], P('section', 'expert'), may hold values from 0 to 1
- router_logits: float32 [64, 1024, 8], P('section', 'expert'), may hold values from -9 to 9
- router_weight: bfloat16 [64, 4096, 8], P('section'), may hold values from -0.59765625 to 0.59765625
Outputs:
- passed_grad: bfloat16 [64, 1024, 4096], P('section', 'expert')
- router_grad: float32 [64, 1024, 8], P('section', 'expert')
Inputs may be any that keep to these rules, and one draw needn't show every extreme that they name: `expert_ids`: the 2 experts of a token differ. `bin_slots`: among the kept choices of the tokens of one device, those of one expert hold distinct slots.
All inputs are finite; a program needn't handle non-finite values.
Results may differ from a plain program's by a relative error of at most 0.003.
Values may be sent and summed in bfloat16 or wider, within the bound.
A program may use at most 64 MiB of HBM per device.

v0:
```python
import jax
import jax.numpy as jnp
from jax import lax
from jax.sharding import PartitionSpec as P


def shifted(shard, axis, by):
    length = lax.axis_size(axis)
    return lax.ppermute(shard, axis, [(i, (i + by) % length) for i in range(length)])


def shards(
    grad_out, expert_outputs, expert_ids, bin_slots, keep_mask, router_logits, router_weight
):
    upstream = grad_out[0]
    binned = expert_outputs[0]
    routed = expert_ids[0]
    slot_ids = bin_slots[0]
    kept_mask = keep_mask[0].astype(jnp.float32)
    logits = router_logits[0]
    weight = router_weight[0]
    groups = lax.axis_size("expert")
    capacity = binned.shape[0] // groups
    columns = upstream.shape[1]
    target = routed * capacity + slot_ids
    parked = jnp.where(keep_mask[0] > 0, target, groups * capacity)
    outgoing = jnp.zeros((groups * capacity, columns), jnp.bfloat16)
    outgoing = outgoing.at[parked[:, 0]].set(upstream, mode="drop")
    outgoing = outgoing.at[parked[:, 1]].set(upstream, mode="drop")
    incoming = lax.all_to_all(
        outgoing.reshape(groups, capacity, columns),
        "expert",
        split_axis=0,
        concat_axis=0,
        tiled=True,
    )
    products = jnp.einsum(
        "scd,scd->sc",
        incoming,
        binned.reshape(groups, capacity, columns),
        preferred_element_type=jnp.float32,
    )
    returned = lax.all_to_all(products, "expert", split_axis=0, concat_axis=0, tiled=True).reshape(
        -1
    )
    inner = returned[target] * kept_mask
    chosen = jnp.take_along_axis(logits, routed, axis=1)
    lead_gate = 1.0 / (1.0 + jnp.exp(chosen[:, 1] - chosen[:, 0]))
    gate_vals = jnp.stack([lead_gate, 1.0 - lead_gate], axis=1)
    gate_mean = jnp.sum(gate_vals * inner, axis=1, keepdims=True)
    chosen_grad = gate_vals * (inner - gate_mean)
    onehot = (routed[:, :, None] == jnp.arange(logits.shape[1])[None, None, :]).astype(jnp.float32)
    logit_grad = jnp.sum(chosen_grad[:, :, None] * onehot, axis=1)
    router_term = jnp.dot(logit_grad, weight.astype(jnp.float32).T, precision=lax.Precision.HIGHEST)
    merged = (upstream.astype(jnp.float32) + router_term).astype(jnp.bfloat16)
    passed = shifted(merged, "section", -1)
    return (passed[None], logit_grad[None])


def solution(mesh):
    in_specs = (
        P("section", "expert", None),
        P("section", "expert", None),
        P("section", "expert", None),
        P("section", "expert", None),
        P("section", "expert", None),
        P("section", "expert", None),
        P("section", None, None),
    )
    out_specs = (P("section", "expert", None), P("section", "expert", None))
    return jax.shard_map(shards, mesh=mesh, in_specs=in_specs, out_specs=out_specs, check_vma=False)
```

profile of v0, /device:TPU:8, one launch (start us, length us, event | category | flops | bytes accessed | tf_op | source)
XLA Modules:
  0.0 100.6 jit_solution(16965626924984788432)
XLA Ops:
  0.6 0.0 copy-start
  0.6 0.7 bitcast_select_fusion
  1.4 3.6 %scatter_custom_fusion = bf16[320,4096]{1,0:T(8,128)(2,1)S(1)} fusion(s32[128]{0:T(128)S(1)} %get-tuple-element.7, bf16[]{:T(256)} %constant.14.clone.1, bf16[1,128,4096]{2,1,0:T(8,128)(2,1)} %param.7), kind=kCustom, calls=%fused_computation.8 | custom fusion | bytes 3670018 | tf_op jit(solution)/shard_map/scatter | solution.py:28
  5.0 4.1 %scatter_custom_fusion.1 = bf16[320,4096]{1,0:T(8,128)(2,1)S(1)} fusion(bf16[320,4096]{1,0:T(8,128)(2,1)S(1)} %scatter_custom_fusion, s32[128]{0:T(128)S(1)} %get-tuple-element.6, bf16[1,128,4096]{2,1,0:T(8,128)(2,1)} %param.7), kind=kCustom, calls=%fused_computation.10 | custom fusion | bytes 3670016 | tf_op jit(solution)/shard_map/scatter | solution.py:29
  9.2 0.0 copy-start.2
  9.2 1.5 %copy-done.2 = bf16[320,4096]{1,0:T(8,128)(2,1)} copy-done((bf16[320,4096]{1,0:T(8,128)(2,1)}, bf16[320,4096]{1,0:T(8,128)(2,1)S(1)}, u32[]{:S(2)}) %copy-start.2) | copy-done | bytes 2621464
  10.7 9.5 %all-to-all-start = ((bf16[8,40,4096]{2,1,0:T(8,128)(2,1)}), bf16[8,40,4096]{2,1,0:T(8,128)(2,1)S(1)}, u32[]{:S(2)}, u32[]{:S(2)}) async-start(bf16[8,40,4096]{2,1,0:T(8,128)(2,1)} %bitcast.49), calls=%async_computation | async-start | bytes 5242880 | tf_op jit(solution)/shard_map/all_to_all | solution.py:30
  20.2 0.0 copy-done.7
  20.2 0.1 copy.44
  20.3 0.1 reshape.125
  20.5 0.1 copy.42
  20.6 0.1 reshape.131
  20.7 1.4 %gather_fusion.1 = f32[256]{0:T(256)S(1)} fusion(f32[128,8]{0,1:T(8,128)S(1)} %bitcast.48, s32[256]{0:T(256)S(1)} %reshape.131), kind=kCustom, calls=%fused_computation.1 | custom fusion | bytes 4096 | tf_op jit(solution)/shard_map/jit(take_along_axis)/gather | solution.py:47
  22.1 0.1 reshape.134
  22.2 0.1 copy.43
  22.3 25.6 %all-to-all-done = bf16[8,40,4096]{2,1,0:T(8,128)(2,1)S(1)} async-done(((bf16[8,40,4096]{2,1,0:T(8,128)(2,1)}), bf16[8,40,4096]{2,1,0:T(8,128)(2,1)S(1)}, u32[]{:S(2)}, u32[]{:S(2)}) %all-to-all-start) | async-done | bytes 2621472 | tf_op jit(solution)/shard_map/all_to_all | solution.py:30
  48.0 3.1 %fusion = f32[8,40]{1,0:T(8,128)} fusion(bf16[8,40,4096]{2,1,0:T(8,128)(2,1)S(1)} %all-to-all-done, bf16[8,40,4096]{2,1,0:T(8,128)(2,1)} %bitcast.50), kind=kLoop, calls=%fused_computation.5 | loop fusion | flops 5242560 | bytes 5244160 | tf_op jit(solution)/shard_map/scd,scd->sc/dot_general | solution.py:37
  51.1 4.4 %all-to-all-start.1 = ((f32[8,1,40]{2,1,0:T(1,128)}), f32[8,1,40]{2,1,0:T(1,128)S(1)}, u32[]{:S(2)}, u32[]{:S(2)}) async-start(f32[8,1,40]{2,1,0:T(1,128)} %bitcast.10), calls=%async_computation.1 | async-start | bytes 8192 | tf_op jit(solution)/shard_map/all_to_all | solution.py:43
  55.5 4.6 %all-to-all-done.1 = f32[8,1,40]{2,1,0:T(1,128)S(1)} async-done(((f32[8,1,40]{2,1,0:T(1,128)}), f32[8,1,40]{2,1,0:T(1,128)S(1)}, u32[]{:S(2)}, u32[]{:S(2)}) %all-to-all-start.1) | async-done | bytes 1312 | tf_op jit(solution)/shard_map/all_to_all | solution.py:43
  60.1 0.5 broadcast.116
  60.7 0.7 reduce.5
  61.3 0.1 reshape.122
  61.4 0.0 copy-start.3
  61.4 1.9 %gather_fusion = f32[256]{0:T(256)S(1)} fusion(f32[320]{0:T(512)S(1)} %reshape.122, s32[1024]{0:T(1024)S(1)} %pad_clamp_fusion), kind=kCustom, calls=%fused_computation | custom fusion | bytes 3072 | tf_op jit(solution)/shard_map/gather | solution.py:46
  63.4 0.1 reshape.124
  63.5 0.1 copy.45
  63.6 0.0 copy-done.6
  63.7 0.0 copy-start.4
  63.7 1.1 %fusion.1 = bf16[128,4096]{1,0:T(8,128)(2,1)S(1)} fusion(f32[128,8]{0,1:T(8,128)S(1)} %select_reduce_fusion, bf16[1,128,4096]{2,1,0:T(8,128)(2,1)S(1)} %copy-done.3, bf16[1,4096,8]{1,2,0:T(8,128)(2,1)S(1)} %copy-done), kind=kOutput, calls=%fused_computation.7 | convolution fusion | flops 51904512 | bytes 2166784 | tf_op jit(solution)/shard_map/dot_general | solution.py:54
  64.7 11.4 %collective-permute-start = (bf16[128,4096]{1,0:T(8,128)(2,1)S(1)}, bf16[128,4096]{1,0:T(8,128)(2,1)S(1)}, u32[]{:S(2)}, u32[]{:S(2)}) collective-permute-start(bf16[128,4096]{1,0:T(8,128)(2,1)S(1)} %fusion.1), channel_id=1, source_target_pairs={{0,504},{8,0},{16,8},{24,16},{32,24},{40,32},{48,40},{56,48},{64,5... | collective-permute-start | bytes 3145736 | tf_op jit(solution)/shard_map/ppermute | solution.py:9
  76.1 23.5 %collective-permute-done = bf16[128,4096]{1,0:T(8,128)(2,1)S(1)} collective-permute-done((bf16[128,4096]{1,0:T(8,128)(2,1)S(1)}, bf16[128,4096]{1,0:T(8,128)(2,1)S(1)}, u32[]{:S(2)}, u32[]{:S(2)}) %collective-permute-start) | collective-permute-done | bytes 1048608 | tf_op jit(solution)/shard_map/ppermute | solution.py:9
  99.6 1.0 copy.53
  (17 shorter events, 0.1 us)
Async XLA Ops:
  0.6 63.0 %copy-start = (bf16[1,4096,8]{1,2,0:T(8,128)(2,1)S(1)}, bf16[1,4096,8]{1,2,0:T(8,128)(2,1)}, u32[]{:S(2)}) copy-start(bf16[1,4096,8]{1,2,0:T(8,128)(2,1)} %param.13) | copy-start | bytes 196612
  9.2 1.5 %copy-start.2 = (bf16[320,4096]{1,0:T(8,128)(2,1)}, bf16[320,4096]{1,0:T(8,128)(2,1)S(1)}, u32[]{:S(2)}) copy-start(bf16[320,4096]{1,0:T(8,128)(2,1)S(1)} %scatter_custom_fusion.1) | copy-start | bytes 7864324
  10.7 9.5 %copy-start.5 = (s32[1,128,2]{1,2,0:T(2,128)S(1)}, s32[1,128,2]{1,2,0:T(2,128)}, u32[]{:S(2)}) copy-start(s32[1,128,2]{1,2,0:T(2,128)} %param.9) | copy-start | bytes 3076
  10.7 9.5 %copy-start.7 = (s32[1,128,2]{1,2,0:T(2,128)S(1)}, s32[1,128,2]{1,2,0:T(2,128)}, u32[]{:S(2)}) copy-start(s32[1,128,2]{1,2,0:T(2,128)} %param.10) | copy-start | bytes 3076
  10.7 10.0 %copy-start.1 = (f32[1,128,8]{1,2,0:T(8,128)S(1)}, f32[1,128,8]{1,2,0:T(8,128)}, u32[]{:S(2)}) copy-start(f32[1,128,8]{1,2,0:T(8,128)} %param.12) | copy-start | bytes 12292
  10.7 37.3 %all-to-all-start = ((bf16[8,40,4096]{2,1,0:T(8,128)(2,1)}), bf16[8,40,4096]{2,1,0:T(8,128)(2,1)S(1)}, u32[]{:S(2)}, u32[]{:S(2)}) async-start(bf16[8,40,4096]{2,1,0:T(8,128)(2,1)} %bitcast.49), calls=%async_computation | async-start | bytes 5242880 | tf_op jit(solution)/shard_map/all_to_all | solution.py:30
  51.1 9.1 %all-to-all-start.1 = ((f32[8,1,40]{2,1,0:T(1,128)}), f32[8,1,40]{2,1,0:T(1,128)S(1)}, u32[]{:S(2)}, u32[]{:S(2)}) async-start(f32[8,1,40]{2,1,0:T(1,128)} %bitcast.10), calls=%async_computation.1 | async-start | bytes 8192 | tf_op jit(solution)/shard_map/all_to_all | solution.py:43
  61.4 2.2 %copy-start.6 = (s32[1,128,2]{1,2,0:T(2,128)S(1)}, s32[1,128,2]{1,2,0:T(2,128)}, u32[]{:S(2)}) copy-start(s32[1,128,2]{1,2,0:T(2,128)} %param.11) | copy-start | bytes 3076
  61.4 2.3 %copy-start.3 = (bf16[1,128,4096]{2,1,0:T(8,128)(2,1)S(1)}, bf16[1,128,4096]{2,1,0:T(8,128)(2,1)}, u32[]{:S(2)}) copy-start(bf16[1,128,4096]{2,1,0:T(8,128)(2,1)} %param.7) | copy-start | bytes 3145732
  63.7 36.9 %copy-start.4 = (f32[128,8]{0,1:T(8,128)}, f32[128,8]{0,1:T(8,128)S(1)}, u32[]{:S(2)}) copy-start(f32[128,8]{0,1:T(8,128)S(1)} %select_reduce_fusion) | copy-start | bytes 12292
  64.7 34.8 %collective-permute-start = (bf16[128,4096]{1,0:T(8,128)(2,1)S(1)}, bf16[128,4096]{1,0:T(8,128)(2,1)S(1)}, u32[]{:S(2)}, u32[]{:S(2)}) collective-permute-start(bf16[128,4096]{1,0:T(8,128)(2,1)S(1)} %fusion.1), channel_id=1, source_target_pairs={{0,504},{8,0},{16,8},{24,16},{32,24},{40,32},{48,40},{56,48},{64,5... | collective-permute-start | bytes 3145736 | tf_op jit(solution)/shard_map/ppermute | solution.py:9
where the time goes:
time: 101 us
  waiting for transfers between devices  53.7 us (53%)
  starting transfers between devices  25.3 us (25%)
  local copies, waits for them, and re-layouts  15.1 us (15%)
  other arithmetic  4.61 us (5%)
  matrix products  1.06 us (1%)
    all_to_all x1, waiting for transfers between devices, shards(): lax.all_to_all(outgoing.reshape(groups, capacity, columns), 'expert', spl...  25.6 us
    ppermute x1, waiting for transfers between devices, shifted(): lax.ppermute(shard, axis, [(i, (i + by) % length) for i in range(length)])  23.5 us
    ppermute x1, starting transfers between devices, shifted(): lax.ppermute(shard, axis, [(i, (i + by) % length) for i in range(length)])  11.4 us
    all_to_all x1, starting transfers between devices, shards(): lax.all_to_all(outgoing.reshape(groups, capacity, columns), 'expert', spl...  9.48 us
    all_to_all x1, waiting for transfers between devices, shards(): lax.all_to_all(products, 'expert', split_axis=0, concat_axis=0, tiled=True)  4.65 us
    all_to_all x1, starting transfers between devices, shards(): lax.all_to_all(products, 'expert', split_axis=0, concat_axis=0, tiled=True)  4.42 us
    scatter x1, local copies, waits for them, and re-layouts, shards(): outgoing = outgoing.at[parked[:, 1]].set(upstream, mode='drop')  4.13 us
    scatter x1, local copies, waits for them, and re-layouts, shards(): outgoing = outgoing.at[parked[:, 0]].set(upstream, mode='drop')  3.63 us
  transfers between devices with their start and end apart: 3, of which 3 were waited for; matrix products, arithmetic and copies ran while one was open for 2% of the time, Pallas kernels for 0%

commit v1 on v0

v1 whole, which is shorter than its diff:
```python
import functools

import jax
import jax.numpy as jnp
from jax import lax
from jax.experimental import pallas as pl
from jax.experimental.pallas import tpu as pltpu
from jax.sharding import PartitionSpec as P

MESH = pl.DeviceIdType.MESH
CHUNKS = 8
F32 = jnp.float32
BF16 = jnp.bfloat16


def kernel(
    caps,
    sections,
    g_hbm,
    e_hbm,
    ids_hbm,
    slots_hbm,
    keep_hbm,
    logits_hbm,
    w_hbm,
    out_ref,
    rg_ref,
    g2,
    ebuf,
    grel,
    ids,
    slots,
    keep,
    logits,
    wrel,
    w3,
    code_own,
    code_par,
    coef,
    coef_rel,
    d_own,
    d_par,
    d_in,
    d_rel_a,
    d_rel_b,
    loc_sem,
    small_send,
    small_recv,
    e_send,
    e_recv,
    x_send,
    x_recv,
    r_send,
    r_recv,
):
    tok = g_hbm.shape[0]
    cols = g_hbm.shape[1]
    span = 2 * caps
    s = lax.axis_index("section")
    e = lax.axis_index("expert")
    core = lax.rem(s, 2)
    x = e // 2
    lo = lax.rem(e, 2)
    partner = (s, e + 1 - 2 * lo)
    before = lax.rem(s + sections - 1, sections)
    after = lax.rem(s + 1, sections)

    local = [
        pltpu.make_async_copy(ids_hbm, ids, loc_sem.at[0]),
        pltpu.make_async_copy(slots_hbm, slots, loc_sem.at[1]),
        pltpu.make_async_copy(keep_hbm, keep, loc_sem.at[2]),
        pltpu.make_async_copy(logits_hbm, logits, loc_sem.at[3]),
        pltpu.make_async_copy(g_hbm, g2.at[pl.ds(0, tok)], loc_sem.at[4]),
    ]
    mine = pl.ds(pl.multiple_of(x * span, 16), span)
    local.append(pltpu.make_async_copy(e_hbm.at[mine], ebuf.at[mine], loc_sem.at[5]))
    for copy in local:
        copy.start()

    barrier = pltpu.get_barrier_semaphore()
    peers = [(s, lax.rem(x + k, 4) * 2 + lo) for k in (1, 2, 3)]
    for source in peers + [partner, (after, e), (after, partner[1])]:
        pl.semaphore_signal(barrier, inc=1, device_id=source, device_id_type=MESH)
    pl.semaphore_wait(barrier, 6)

    def remote(src, dst, send, recv, device):
        return pltpu.make_async_remote_copy(
            src_ref=src, dst_ref=dst, send_sem=send, recv_sem=recv, device_id=device, device_id_type=MESH
        )

    rows = tok // CHUNKS
    exchange = [
        remote(
            g_hbm.at[pl.ds(i * rows, rows)],
            g2.at[pl.ds(tok + i * rows, rows)],
            x_send.at[i],
            x_recv.at[i],
            partner,
        )
        for i in range(CHUNKS)
    ]
    for copy in exchange:
        copy.start()
    experts = []
    for k, peer in enumerate(peers):
        theirs = pl.ds(pl.multiple_of(lax.rem(x + k + 1, 4) * span, 16), span)
        experts.append(remote(e_hbm.at[theirs], ebuf.at[mine], e_send.at[k], e_recv.at[k], peer))
        experts[-1].start()
    relay = remote(g_hbm, grel, r_send.at[0], r_recv, (before, e))
    direct = jnp.logical_or(core == 1, lo == 0)
    forwards = jnp.logical_and(core == 0, lo == 0)

    @pl.when(direct)
    def _():
        relay.start()

    weight = remote(w_hbm, wrel, small_send.at[0], small_recv.at[0], (before, e))
    weight.start()

    for copy in local[:4]:
        copy.wait()
    code = jnp.where(keep[...] > 0, ids[...] * caps + slots[...], -1)
    code_own[...] = code
    codes = remote(code_own, code_par, small_send.at[1], small_recv.at[1], partner)
    codes.start()
    experts_n = logits.shape[0]
    row = lax.broadcasted_iota(jnp.int32, (experts_n, tok), 0)
    first = (row == ids[0:1, :]).astype(F32)
    second = (row == ids[1:2, :]).astype(F32)
    gap = jnp.sum(logits[...] * (second - first), axis=0, keepdims=True)
    lead = 1.0 / (1.0 + jnp.exp(gap))
    coef[...] = lead * (1.0 - lead) * (first - second)
    coefs = remote(coef, coef_rel, small_send.at[2], small_recv.at[2], (before, e))
    coefs.start()

    for copy in local[4:]:
        copy.wait()
    forward = [
        remote(
            g2.at[pl.ds(tok + i * rows, rows)],
            grel.at[pl.ds(i * rows, rows)],
            r_send.at[i + 1],
            r_recv,
            (before, partner[1]),
        )
        for i in range(CHUNKS)
    ]
    for i in range(CHUNKS):
        exchange[i].wait_recv()

        @pl.when(forwards)
        def _():
            forward[i].start()

    weight.wait_recv()
    wide = wrel[...].astype(F32)
    w3[...] = jnp.concatenate([wide, wide, wide, jnp.zeros_like(wide)], axis=0).astype(BF16)
    codes.wait_recv()
    for copy in experts:
        copy.wait_recv()

    def part(first_row, codes_ref, tok_lo):
        sums = lax.dot_general(
            ebuf[...],
            g2[first_row : first_row + tok, :],
            (((1,), (1,)), ((), ())),
            preferred_element_type=F32,
        )
        total = jnp.zeros((1, tok), F32)
        for k in range(4):
            at = lax.broadcasted_iota(jnp.int32, (span, tok), 0) - tok_lo * caps
            inside = jnp.logical_and(at >= 0, at < caps)
            want = jnp.where(inside, at + (2 * k + lo) * caps, -2)
            block = sums[k * span : (k + 1) * span]
            total += jnp.sum(
                jnp.where(want == codes_ref[0:1, :], block, 0.0)
                - jnp.where(want == codes_ref[1:2, :], block, 0.0),
                axis=0,
                keepdims=True,
            )
        return jnp.broadcast_to(total, (8, tok))

    d_par[...] = part(tok, code_par, 1 - lo)
    back = remote(d_par, d_in, small_send.at[3], small_recv.at[3], partner)
    back.start()
    on = remote(d_par, d_rel_b, small_send.at[4], small_recv.at[4], (before, partner[1]))
    on.start()
    d_own[...] = part(0, code_own, lo)
    own = remote(d_own, d_rel_a, small_send.at[5], small_recv.at[5], (before, e))
    own.start()

    back.wait_recv()
    rg_ref[...] = coef[...] * (d_own[...] + d_in[...])

    coefs.wait_recv()
    on.wait_recv()
    own.wait_recv()
    grad = coef_rel[...] * (d_rel_a[...] + d_rel_b[...])
    high = grad.astype(BF16)
    rest = grad - high.astype(F32)
    mid = rest.astype(BF16)
    low = rest - mid.astype(F32)
    pieces = jnp.concatenate([high.astype(F32), mid.astype(F32), low, jnp.zeros_like(low)], axis=0)
    left = pieces.T.astype(BF16)
    relay.wait_recv()
    step = 512
    for at in range(0, cols, step):
        term = jnp.dot(left, w3[:, at : at + step], preferred_element_type=F32)
        out_ref[:, at : at + step] = (grel[:, at : at + step].astype(F32) + term).astype(BF16)

    for copy in exchange + experts + [weight, codes, coefs, back, on, own]:
        copy.wait_send()

    @pl.when(direct)
    def _():
        relay.wait_send()

    @pl.when(forwards)
    def _():
        for copy in forward:
            copy.wait_send()


def shards(
    grad_out, expert_outputs, expert_ids, bin_slots, keep_mask, router_logits, router_weight
):
    tok, cols = grad_out.shape[1:]
    experts_n = router_logits.shape[2]
    caps = expert_outputs.shape[1] // experts_n
    dma = pltpu.SemaphoreType.DMA
    passed, grad = pl.pallas_call(
        functools.partial(kernel, caps, lax.axis_size("section")),
        out_shape=(
            jax.ShapeDtypeStruct((tok, cols), BF16),
            jax.ShapeDtypeStruct((experts_n, tok), F32),
        ),
        in_specs=[pl.BlockSpec(memory_space=pltpu.HBM)] * 7,
        out_specs=(pl.BlockSpec(memory_space=pltpu.VMEM), pl.BlockSpec(memory_space=pltpu.VMEM)),
        scratch_shapes=[
            pltpu.VMEM((2 * tok, cols), BF16),
            pltpu.VMEM((8 * caps, cols), BF16),
            pltpu.VMEM((tok, cols), BF16),
            pltpu.VMEM((2, tok), jnp.int32),
            pltpu.VMEM((2, tok), jnp.int32),
            pltpu.VMEM((2, tok), jnp.int32),
            pltpu.VMEM((experts_n, tok), F32),
            pltpu.VMEM((experts_n, cols), BF16),
            pltpu.VMEM((4 * experts_n, cols), BF16),
            pltpu.VMEM((2, tok), jnp.int32),
            pltpu.VMEM((2, tok), jnp.int32),
            pltpu.VMEM((experts_n, tok), F32),
            pltpu.VMEM((experts_n, tok), F32),
            pltpu.VMEM((8, tok), F32),
            pltpu.VMEM((8, tok), F32),
            pltpu.VMEM((8, tok), F32),
            pltpu.VMEM((8, tok), F32),
            pltpu.VMEM((8, tok), F32),
            dma((6,)),
            dma((6,)),
            dma((6,)),
            dma((3,)),
            dma((3,)),
            dma((CHUNKS,)),
            dma((CHUNKS,)),
            dma((CHUNKS + 1,)),
            dma,
        ],
        compiler_params=pltpu.CompilerParams(
            collective_id=0, has_side_effects=True, vmem_limit_bytes=62 << 20
        ),
        cost_estimate=pl.CostEstimate(flops=700_000_000, bytes_accessed=8_000_000, transcendentals=128),
        name="combine_router_backward",
    )(
        grad_out[0],
        expert_outputs[0],
        expert_ids[0].T,
        bin_slots[0].T,
        keep_mask[0].T,
        router_logits[0].T,
        router_weight[0].T,
    )
    return (passed[None], grad.T[None])


def solution(mesh):
    in_specs = (
        P("section", "expert", None),
        P("section", "expert", None),
        P("section", "expert", None),
        P("section", "expert", None),
        P("section", "expert", None),
        P("section", "expert", None),
        P("section", None, None),
    )
    out_specs = (P("section", "expert", None), P("section", "expert", None))
    return jax.shard_map(shards, mesh=mesh, in_specs=in_specs, out_specs=out_specs, check_vma=False)
```

time: 101 us -> 55.5 us (0.55)
  the two profiles are of different devices: /device:TPU:8 before, /device:TPU:1 now
where the time goes in v1:
time: 55.5 us; the launch traced here: 55.3 us
  Pallas kernels  51.1 us (92%)
  local copies, waits for them, and re-layouts  3.56 us (6%)
  between operations  0.64 us (1%)
    pallas_call x1, Pallas kernels, shards(): pl.pallas_call(functools.partial(kernel, caps, lax.axis_size('section')),...  51.1 us
    unnamed x2, local copies, waits for them, and re-layouts  3.56 us

profile of v1, /device:TPU:1, one launch (start us, length us, event | category | flops | bytes accessed | tf_op | source)
XLA Modules:
  0.0 55.3 jit_solution(13412032457365448848)
XLA Ops:
  0.6 51.1 %combine_router_backward.1 = (bf16[128,4096]{1,0:T(8,128)(2,1)}, f32[8,128]{1,0:T(8,128)}) custom-call(bf16[128,4096]{1,0:T(8,128)(2,1)} %bitcast.22, bf16[320,4096]{1,0:T(8,128)(2,1)} %bitcast.21, s32[2,128]{1,0:T(2,128)} %bitcast.27, s32[2,128]{1,0:T(2,128)} %bitcast.28, s32[2,128]{1,0:T(2,128)} %bitcast.29, f32[8,128]{1,0:T(8,128)} %bitcast.25, ...), custom_call_target="tpu_custom_call" | custom-call | flops 700000000 | bytes 8000000 | tf_op jit(solution)/shard_map/combine_router_backward/pallas_call | solution.py:231
  51.7 2.3 %copy.11 = bf16[1,128,4096]{2,1,0:T(8,128)(2,1)} copy(bf16[1,128,4096]{2,1,0:T(8,128)(2,1)} %bitcast.23) | data formatting | bytes 2097152
  54.0 1.3 %copy.12 = f32[1,128,8]{1,2,0:T(8,128)} copy(f32[1,128,8]{1,2,0:T(8,128)} %bitcast.26) | data formatting | bytes 8192

commit v2 on v1

--- a/solution.py
+++ b/solution.py
@@ -9,6 +9,9 @@
 
 MESH = pl.DeviceIdType.MESH
 CHUNKS = 8
+FIRST = 2
+SHARE = 3
+LAUNCH = ((),(),(),(),(),(),(),(0,1,2,3,4,5,6,7))
 F32 = jnp.float32
 BF16 = jnp.bfloat16
 
@@ -28,6 +31,8 @@
     g2,
     ebuf,
     grel,
+    hbuf,
+    e2,
     ids,
     slots,
     keep,
@@ -51,7 +56,12 @@
     x_send,
     x_recv,
     r_send,
+    o_send,
     r_recv,
+    h_sem,
+    c_send,
+    c_recv,
+    go_sem,
 ):
     tok = g_hbm.shape[0]
     cols = g_hbm.shape[1]
@@ -65,6 +75,40 @@
     before = lax.rem(s + sections - 1, sections)
     after = lax.rem(s + 1, sections)
 
+    barrier = pltpu.get_barrier_semaphore()
+    peers = [(s, lax.rem(x + k, 4) * 2 + lo) for k in (1, 2, 3)]
+    helper = jnp.logical_and(core == 1, lo == 0)
+    helped = jnp.logical_and(core == 0, lo == 0)
+    taker = jnp.logical_and(core == 1, lo == 1)
+    across = [(s, lax.rem(x + k, 4) * 2 + 1 - lo) for k in (1, 2, 3)]
+    behind = lax.rem(s + sections - 2, sections)
+
+    def greet(devices, semaphore):
+        for device in devices:
+            pl.semaphore_signal(semaphore, inc=1, device_id=device, device_id_type=MESH)
+
+    greet(peers + [partner], barrier)
+
+    @pl.when(core == 0)
+    def _():
+        greet([(after, e), (after, partner[1]), (before, e), (before, partner[1])], barrier)
+        pl.semaphore_wait(barrier, 4)
+
+    @pl.when(core == 1)
+    def _():
+        @pl.when(lo == 0)
+        def _():
+            greet([(lax.rem(s + 2, sections), e)], barrier)
+            pl.semaphore_wait(barrier, 12)
+            greet([(before, e)], go_sem)
+
+        @pl.when(lo == 1)
+        def _():
+            greet(across, barrier)
+            pl.semaphore_wait(barrier, 8)
+
+        greet([(after, e), (after, partner[1])], go_sem)
+
     local = [
         pltpu.make_async_copy(ids_hbm, ids, loc_sem.at[0]),
         pltpu.make_async_copy(slots_hbm, slots, loc_sem.at[1]),
@@ -77,40 +121,93 @@
     for copy in local:
         copy.start()
 
-    barrier = pltpu.get_barrier_semaphore()
-    peers = [(s, lax.rem(x + k, 4) * 2 + lo) for k in (1, 2, 3)]
-    for source in peers + [partner, (after, e), (after, partner[1])]:
-        pl.semaphore_signal(barrier, inc=1, device_id=source, device_id_type=MESH)
-    pl.semaphore_wait(barrier, 6)
-
     def remote(src, dst, send, recv, device):
         return pltpu.make_async_remote_copy(
             src_ref=src, dst_ref=dst, send_sem=send, recv_sem=recv, device_id=device, device_id_type=MESH
         )
 
     rows = tok // CHUNKS
-    exchange = [
-        remote(
-            g_hbm.at[pl.ds(i * rows, rows)],
-            g2.at[pl.ds(tok + i * rows, rows)],
+    cut = cols // 8 * SHARE
+
+    def swap(i, first):
+        return remote(
+            g_hbm.at[pl.ds(i * rows, rows), pl.ds(first, cols - first)],
+            g2.at[pl.ds(tok + i * rows, rows), pl.ds(first, cols - first)],
             x_send.at[i],
             x_recv.at[i],
             partner,
         )
-        for i in range(CHUNKS)
-    ]
-    for copy in exchange:
-        copy.start()
-    experts = []
-    for k, peer in enumerate(peers):
-        theirs = pl.ds(pl.multiple_of(lax.rem(x + k + 1, 4) * span, 16), span)
-        experts.append(remote(e_hbm.at[theirs], ebuf.at[mine], e_send.at[k], e_recv.at[k], peer))
-        experts[-1].start()
+
+    exchange = [swap(i, 0) for i in range(CHUNKS)]
+    shorter = [swap(i, cut) for i in range(CHUNKS)]
+
+    @pl.when(taker)
+    def _():
+        for copy in shorter:
+            copy.start()
+
+    @pl.when(jnp.logical_not(taker))
+    def _():
+        for copy in exchange:
+            copy.start()
+
+    lead_rows = caps // 16 * 16 + 16
+
+    def rows_to(k, first, count, from_col):
+        theirs = pl.ds(pl.multiple_of(lax.rem(x + k + 1, 4) * span + first, 16), count)
+        here = pl.ds(pl.multiple_of(x * span + first, 16), count)
+        return remote(
+            e_hbm.at[theirs, pl.ds(from_col, cols - from_col)],
+            ebuf.at[here, pl.ds(from_col, cols - from_col)],
+            e_send.at[k + (3 if first else 0)],
+            e_recv.at[k + (3 if first else 0)],
+            peers[k],
+        )
+
+    experts = [rows_to(k, 0, span, 0) for k in range(3)]
+    experts_lead = [rows_to(k, 0, lead_rows, 0) for k in range(3)]
+    experts_rest = [rows_to(k, lead_rows, span - lead_rows, cut) for k in range(3)]
+    second = span - lead_rows
+
+    def rows_across(k):
+        at = x if k == 3 else lax.rem(x + k + 1, 4)
+        return remote(
+            e_hbm.at[pl.ds(pl.multiple_of(at * span + second, 16), lead_rows), pl.ds(0, cut)],
+            e2.at[pl.ds(pl.multiple_of(x * lead_rows, 16), lead_rows)],
+            c_send.at[k],
+            c_recv.at[k],
+            partner if k == 3 else across[k],
+        )
+
+    crossing = [rows_across(k) for k in range(4)]
+
+    @pl.when(helper)
+    def _():
+        for copy in experts_lead + experts_rest + crossing:
+            copy.start()
+
+    @pl.when(jnp.logical_not(helper))
+    def _():
+        for copy in experts:
+            copy.start()
+
+    @pl.when(helped)
+    def _():
+        pl.semaphore_wait(go_sem, 3)
+
+    @pl.when(jnp.logical_and(core == 0, lo == 1))
+    def _():
+        pl.semaphore_wait(go_sem, 2)
+
     relay = remote(g_hbm, grel, r_send.at[0], r_recv, (before, e))
-    direct = jnp.logical_or(core == 1, lo == 0)
-    forwards = jnp.logical_and(core == 0, lo == 0)
-
-    @pl.when(direct)
+    inside = core == 1
+    help_out = remote(g_hbm, hbuf, h_sem.at[0], h_sem.at[1], (after, e))
+
+    @pl.when(helped)
+    def _():
+        help_out.start()
+
+    @pl.when(inside)
     def _():
         relay.start()
 
@@ -126,10 +223,10 @@
     experts_n = logits.shape[0]
     row = lax.broadcasted_iota(jnp.int32, (experts_n, tok), 0)
     first = (row == ids[0:1, :]).astype(F32)
-    second = (row == ids[1:2, :]).astype(F32)
-    gap = jnp.sum(logits[...] * (second - first), axis=0, keepdims=True)
+    second_is = (row == ids[1:2, :]).astype(F32)
+    gap = jnp.sum(logits[...] * (second_is - first), axis=0, keepdims=True)
     lead = 1.0 / (1.0 + jnp.exp(gap))
-    coef[...] = lead * (1.0 - lead) * (first - second)
+    coef[...] = lead * (1.0 - lead) * (first - second_is)
     coefs = remote(coef, coef_rel, small_send.at[2], small_recv.at[2], (before, e))
     coefs.start()
 
@@ -145,47 +242,105 @@
         )
         for i in range(CHUNKS)
     ]
+    outward = [
+        remote(
+            hbuf.at[pl.ds(i * rows, rows)],
+            grel.at[pl.ds(i * rows, rows)],
+            o_send.at[i],
+            r_recv,
+            (behind, e),
+        )
+        for i in range(CHUNKS)
+    ]
     for i in range(CHUNKS):
-        exchange[i].wait_recv()
-
-        @pl.when(forwards)
+        if i == FIRST:
+
+            @pl.when(helper)
+            def _():
+                help_out.wait_recv()
+
+        @pl.when(helper)
+        def _():
+            shorter[i].wait_recv()
+
+        @pl.when(jnp.logical_not(helper))
+        def _():
+            exchange[i].wait_recv()
+
+        @pl.when(helped)
         def _():
             forward[i].start()
+
+        @pl.when(helper)
+        def _():
+            for j in LAUNCH[i]:
+                outward[j].start()
 
     weight.wait_recv()
     wide = wrel[...].astype(F32)
     w3[...] = jnp.concatenate([wide, wide, wide, jnp.zeros_like(wide)], axis=0).astype(BF16)
     codes.wait_recv()
-    for copy in experts:
-        copy.wait_recv()
-
-    def part(first_row, codes_ref, tok_lo):
+
+    d_own[...] = jnp.zeros_like(d_own)
+    d_par[...] = jnp.zeros_like(d_par)
+
+    def add(into, held, first_row, first_col, last_col, want, codes_ref):
         sums = lax.dot_general(
-            ebuf[...],
-            g2[first_row : first_row + tok, :],
+            held,
+            g2[first_row : first_row + tok, first_col:last_col],
             (((1,), (1,)), ((), ())),
             preferred_element_type=F32,
         )
-        total = jnp.zeros((1, tok), F32)
-        for k in range(4):
-            at = lax.broadcasted_iota(jnp.int32, (span, tok), 0) - tok_lo * caps
-            inside = jnp.logical_and(at >= 0, at < caps)
-            want = jnp.where(inside, at + (2 * k + lo) * caps, -2)
-            block = sums[k * span : (k + 1) * span]
-            total += jnp.sum(
-                jnp.where(want == codes_ref[0:1, :], block, 0.0)
-                - jnp.where(want == codes_ref[1:2, :], block, 0.0),
-                axis=0,
-                keepdims=True,
-            )
-        return jnp.broadcast_to(total, (8, tok))
-
-    d_par[...] = part(tok, code_par, 1 - lo)
+        total = jnp.sum(
+            jnp.where(want == codes_ref[0:1, :], sums, 0.0)
+            - jnp.where(want == codes_ref[1:2, :], sums, 0.0),
+            axis=0,
+            keepdims=True,
+        )
+        into[...] += jnp.broadcast_to(total, into.shape)
+
+    def wanted(at, tok_lo):
+        slot = lax.broadcasted_iota(jnp.int32, (span, tok), 0) - tok_lo * caps
+        ours = jnp.logical_and(slot >= 0, slot < caps)
+        return jnp.where(ours, slot + (2 * at + lo) * caps, -2)
+
+    def block(at):
+        here = pl.ds(pl.multiple_of(at * span, 16), span)
+        add(d_own, ebuf[here, :], 0, 0, cols, wanted(at, lo), code_own)
+        theirs = wanted(at, 1 - lo)
+        add(d_par, ebuf[here, cut:], tok, cut, cols, theirs, code_par)
+
+        @pl.when(jnp.logical_not(helper))
+        def _():
+            add(d_par, ebuf[here, :cut], tok, 0, cut, theirs, code_par)
+
+    block(x)
+    for k in (0, 2, 1):
+
+        @pl.when(helper)
+        def _():
+            experts_lead[k].wait_recv()
+            experts_rest[k].wait_recv()
+
+        @pl.when(jnp.logical_not(helper))
+        def _():
+            experts[k].wait_recv()
+
+        block(lax.rem(x + 3 - k, 4))
+
+    @pl.when(taker)
+    def _():
+        for copy in crossing:
+            copy.wait_recv()
+        for at in range(4):
+            slot = lax.broadcasted_iota(jnp.int32, (lead_rows, tok), 0) - (caps - second)
+            want = jnp.where(slot >= 0, slot + 2 * at * caps, -2)
+            add(d_own, e2[at * lead_rows : (at + 1) * lead_rows, :], 0, 0, cut, want, code_own)
+
     back = remote(d_par, d_in, small_send.at[3], small_recv.at[3], partner)
     back.start()
     on = remote(d_par, d_rel_b, small_send.at[4], small_recv.at[4], (before, partner[1]))
     on.start()
-    d_own[...] = part(0, code_own, lo)
     own = remote(d_own, d_rel_a, small_send.at[5], small_recv.at[5], (before, e))
     own.start()
 
@@ -208,16 +363,41 @@
         term = jnp.dot(left, w3[:, at : at + step], preferred_element_type=F32)
         out_ref[:, at : at + step] = (grel[:, at : at + step].astype(F32) + term).astype(BF16)
 
-    for copy in exchange + experts + [weight, codes, coefs, back, on, own]:
+    for copy in [weight, codes, coefs, back, on, own]:
         copy.wait_send()
 
-    @pl.when(direct)
+    @pl.when(taker)
+    def _():
+        for copy in shorter:
+            copy.wait_send()
+
+    @pl.when(jnp.logical_not(taker))
+    def _():
+        for copy in exchange:
+            copy.wait_send()
+
+    @pl.when(helper)
+    def _():
+        for copy in experts_lead + experts_rest + crossing:
+            copy.wait_send()
+
+    @pl.when(jnp.logical_not(helper))
+    def _():
+        for copy in experts:
+            copy.wait_send()
+
+    @pl.when(inside)
     def _():
         relay.wait_send()
 
-    @pl.when(forwards)
-    def _():
-        for copy in forward:
+    @pl.when(helped)
+    def _():
+        for copy in forward + [help_out]:
+            copy.wait_send()
+
+    @pl.when(helper)
+    def _():
+        for copy in outward:
             copy.wait_send()
 
 
@@ -240,6 +420,8 @@
             pltpu.VMEM((2 * tok, cols), BF16),
             pltpu.VMEM((8 * caps, cols), BF16),
             pltpu.VMEM((tok, cols), BF16),
+            pltpu.VMEM((tok, cols), BF16),
+            pltpu.VMEM((4 * (caps // 16 * 16 + 16), cols // 8 * SHARE), BF16),
             pltpu.VMEM((2, tok), jnp.int32),
             pltpu.VMEM((2, tok), jnp.int32),
             pltpu.VMEM((2, tok), jnp.int32),
@@ -258,26 +440,36 @@
             dma((6,)),
             dma((6,)),
             dma((6,)),
-            dma((3,)),
-            dma((3,)),
+            dma((6,)),
+            dma((6,)),
             dma((CHUNKS,)),
             dma((CHUNKS,)),
             dma((CHUNKS + 1,)),
+            dma((CHUNKS,)),
             dma,
+            dma((2,)),
+            dma((4,)),
+            dma((4,)),
+            pltpu.SemaphoreType.REGULAR,
         ],
         compiler_params=pltpu.CompilerParams(
-            collective_id=0, has_side_effects=True, vmem_limit_bytes=62 << 20
+            collective_id=0, has_side_effects=True, vmem_limit_bytes=40 << 20
         ),
         cost_estimate=pl.CostEstimate(flops=700_000_000, bytes_accessed=8_000_000, transcendentals=128),
         name="combine_router_backward",
     )(
-        grad_out[0],
-        expert_outputs[0],
-        expert_ids[0].T,
-        bin_slots[0].T,
-        keep_mask[0].T,
-        router_logits[0].T,
-        router_weight[0].T,
+        *(
+            pltpu.with_memory_space_constraint(operand, pltpu.HBM)
+            for operand in (
+                grad_out[0],
+                expert_outputs[0],
+                expert_ids[0].T,
+                bin_slots[0].T,
+                keep_mask[0].T,
+                router_logits[0].T,
+                router_weight[0].T,
+            )
+        )
     )
     return (passed[None], grad.T[None])
 

time: 55.5 us -> 49.2 us (0.89)
  Pallas kernels: 51.1 us -> 46.9 us
  local copies, waits for them, and re-layouts: 3.56 us -> 1.56 us
    pallas_call x1, Pallas kernels: 51.1 us -> 46.9 us  [shards(): pl.pallas_call(functools.partial(kernel, caps, lax.axis_size('section')),...]
    unnamed x2, local copies, waits for them, and re-layouts: 3.56 us -> 1.56 us
where the time goes in v2:
time: 49.2 us; the launch traced here: 49.1 us
  Pallas kernels  46.9 us (95%)
  local copies, waits for them, and re-layouts  1.56 us (3%)
  between operations  0.64 us (1%)
    pallas_call x1, Pallas kernels, shards(): pl.pallas_call(functools.partial(kernel, caps, lax.axis_size('section')),...  46.9 us
    unnamed x2, local copies, waits for them, and re-layouts  1.56 us

profile of v2, /device:TPU:1, one launch (start us, length us, event | category | flops | bytes accessed | tf_op | source)
XLA Modules:
  0.0 49.1 jit_solution(320339876965016976)
XLA Ops:
  0.6 46.9 %combine_router_backward.1 = (bf16[128,4096]{1,0:T(8,128)(2,1)S(1)}, f32[8,128]{1,0:T(8,128)S(1)}) custom-call(bf16[128,4096]{1,0:T(8,128)(2,1)} %bitcast.24, bf16[320,4096]{1,0:T(8,128)(2,1)} %bitcast.23, s32[2,128]{1,0:T(2,128)} %bitcast.27, s32[2,128]{1,0:T(2,128)} %bitcast.28, s32[2,128]{1,0:T(2,128)} %bitcast.29, f32[8,128]{1,0:T(8,128)} %bitcast.26, ...), custom_call_target="tpu_custom_call" | custom-call | flops 700000000 | bytes 8000000 | tf_op jit(solution)/shard_map/combine_router_backward/pallas_call | solution.py:411
  47.5 1.0 %copy.11 = bf16[1,128,4096]{2,1,0:T(8,128)(2,1)} copy(bf16[1,128,4096]{2,1,0:T(8,128)(2,1)S(1)} %bitcast.21) | data formatting | bytes 2097152
  48.5 0.6 %copy.12 = f32[1,128,8]{1,2,0:T(8,128)} copy(f32[1,128,8]{1,2,0:T(8,128)S(1)} %bitcast.22) | data formatting | bytes 8192

commit v3 on v2

--- a/solution.py
+++ b/solution.py
@@ -9,9 +9,11 @@
 
 MESH = pl.DeviceIdType.MESH
 CHUNKS = 8
-FIRST = 2
-SHARE = 3
-LAUNCH = ((),(),(),(),(),(),(),(0,1,2,3,4,5,6,7))
+FORWARD = 4
+BESIDE = 3
+FIRST = 5
+SECOND = 5
+SHARE = 1
 F32 = jnp.float32
 BF16 = jnp.bfloat16
 
@@ -39,12 +41,10 @@
     logits,
     wrel,
     w3,
-    code_own,
-    code_par,
+    code_all,
     coef,
     coef_rel,
-    d_own,
-    d_par,
+    d_all,
     d_in,
     d_rel_a,
     d_rel_b,
@@ -56,9 +56,9 @@
     x_send,
     x_recv,
     r_send,
-    o_send,
     r_recv,
-    h_sem,
+    h_send,
+    h_recv,
     c_send,
     c_recv,
     go_sem,
@@ -77,11 +77,10 @@
 
     barrier = pltpu.get_barrier_semaphore()
     peers = [(s, lax.rem(x + k, 4) * 2 + lo) for k in (1, 2, 3)]
-    helper = jnp.logical_and(core == 1, lo == 0)
-    helped = jnp.logical_and(core == 0, lo == 0)
-    taker = jnp.logical_and(core == 1, lo == 1)
+    even = lo == 0
+    c0_even, c0_odd = jnp.logical_and(core == 0, even), jnp.logical_and(core == 0, lo == 1)
+    c1_even, c1_odd = jnp.logical_and(core == 1, even), jnp.logical_and(core == 1, lo == 1)
     across = [(s, lax.rem(x + k, 4) * 2 + 1 - lo) for k in (1, 2, 3)]
-    behind = lax.rem(s + sections - 2, sections)
 
     def greet(devices, semaphore):
         for device in devices:
@@ -96,16 +95,15 @@
 
     @pl.when(core == 1)
     def _():
-        @pl.when(lo == 0)
-        def _():
-            greet([(lax.rem(s + 2, sections), e)], barrier)
-            pl.semaphore_wait(barrier, 12)
-            greet([(before, e)], go_sem)
-
         @pl.when(lo == 1)
         def _():
             greet(across, barrier)
             pl.semaphore_wait(barrier, 8)
+
+        @pl.when(even)
+        def _():
+            pl.semaphore_wait(barrier, 11)
+            greet([(before, partner[1])], go_sem)
 
         greet([(after, e), (after, partner[1])], go_sem)
 
@@ -141,12 +139,12 @@
     exchange = [swap(i, 0) for i in range(CHUNKS)]
     shorter = [swap(i, cut) for i in range(CHUNKS)]
 
-    @pl.when(taker)
+    @pl.when(c1_odd)
     def _():
         for copy in shorter:
             copy.start()
 
-    @pl.when(jnp.logical_not(taker))
+    @pl.when(jnp.logical_not(c1_odd))
     def _():
         for copy in exchange:
             copy.start()
@@ -181,31 +179,42 @@
 
     crossing = [rows_across(k) for k in range(4)]
 
-    @pl.when(helper)
+    @pl.when(c1_even)
     def _():
         for copy in experts_lead + experts_rest + crossing:
             copy.start()
 
-    @pl.when(jnp.logical_not(helper))
+    @pl.when(jnp.logical_not(c1_even))
     def _():
         for copy in experts:
             copy.start()
 
-    @pl.when(helped)
+    @pl.when(c0_even)
+    def _():
+        pl.semaphore_wait(go_sem, 2)
+
+    @pl.when(c0_odd)
     def _():
         pl.semaphore_wait(go_sem, 3)
-
-    @pl.when(jnp.logical_and(core == 0, lo == 1))
-    def _():
-        pl.semaphore_wait(go_sem, 2)
 
     relay = remote(g_hbm, grel, r_send.at[0], r_recv, (before, e))
     inside = core == 1
-    help_out = remote(g_hbm, hbuf, h_sem.at[0], h_sem.at[1], (after, e))
-
-    @pl.when(helped)
-    def _():
-        help_out.start()
+    half = tok // 2
+    halves = [pl.ds(0, half), pl.ds(half, half)]
+    hops = [
+        remote(g_hbm.at[part], hbuf.at[part], h_send.at[k], h_recv.at[k], (before, partner[1]))
+        for k, part in enumerate(halves)
+    ]
+    beside = remote(hbuf.at[halves[0]], hbuf.at[halves[0]], h_send.at[2], h_recv.at[2], (before, e))
+    ends = [
+        remote(hbuf.at[halves[1]], grel.at[halves[1]], h_send.at[3], r_recv, partner),
+        remote(hbuf.at[halves[0]], grel.at[halves[0]], h_send.at[4], r_recv, (after, partner[1])),
+    ]
+
+    @pl.when(c0_even)
+    def _():
+        for copy in hops:
+            copy.start()
 
     @pl.when(inside)
     def _():
@@ -217,8 +226,9 @@
     for copy in local[:4]:
         copy.wait()
     code = jnp.where(keep[...] > 0, ids[...] * caps + slots[...], -1)
-    code_own[...] = code
-    codes = remote(code_own, code_par, small_send.at[1], small_recv.at[1], partner)
+    ours, theirs = pl.ds(0, tok), pl.ds(tok, tok)
+    code_all[:, ours] = code
+    codes = remote(code_all.at[:, ours], code_all.at[:, theirs], small_send.at[1], small_recv.at[1], partner)
     codes.start()
     experts_n = logits.shape[0]
     row = lax.broadcasted_iota(jnp.int32, (experts_n, tok), 0)
@@ -232,6 +242,46 @@
 
     for copy in local[4:]:
         copy.wait()
+    d_all[...] = jnp.zeros_like(d_all)
+    lane = lax.broadcasted_iota(jnp.int32, (span, 2 * tok), 1)
+    slot = lax.broadcasted_iota(jnp.int32, (span, 2 * tok), 0) - jnp.where(lane < tok, lo, 1 - lo) * caps
+    held_here = jnp.logical_and(slot >= 0, slot < caps)
+
+    def wanted(at):
+        return jnp.where(held_here, slot + (2 * at + lo) * caps, -2)
+
+    def block_rows(at):
+        return pl.ds(pl.multiple_of(at * span, 16), span)
+
+    def product(held, first, last, first_col, last_col):
+        return lax.dot_general(
+            held, g2[first:last, first_col:last_col], (((1,), (1,)), ((), ())), preferred_element_type=F32
+        )
+
+    def pick(first, last, sums, want):
+        total = jnp.sum(
+            jnp.where(want == code_all[0:1, first:last], sums, 0.0)
+            - jnp.where(want == code_all[1:2, first:last], sums, 0.0),
+            axis=0,
+            keepdims=True,
+        )
+        d_all[:, first:last] += jnp.broadcast_to(total, (8, last - first))
+
+    def add(first, last, held, first_col, last_col, want):
+        pick(first, last, product(held, first, last, first_col, last_col), want[:, first:last])
+
+    def add_both(rows_at, want):
+        @pl.when(c1_even)
+        def _():
+            add(0, 2 * tok, ebuf[rows_at, cut:], cut, cols, want)
+            add(0, tok, ebuf[rows_at, :cut], 0, cut, want)
+
+        @pl.when(jnp.logical_not(c1_even))
+        def _():
+            add(0, 2 * tok, ebuf[rows_at, :], 0, cols, want)
+
+    add(0, tok, ebuf[block_rows(x), :], 0, cols, wanted(x))
+
     forward = [
         remote(
             g2.at[pl.ds(tok + i * rows, rows)],
@@ -242,110 +292,99 @@
         )
         for i in range(CHUNKS)
     ]
-    outward = [
-        remote(
-            hbuf.at[pl.ds(i * rows, rows)],
-            grel.at[pl.ds(i * rows, rows)],
-            o_send.at[i],
-            r_recv,
-            (behind, e),
-        )
-        for i in range(CHUNKS)
-    ]
     for i in range(CHUNKS):
+        @pl.when(c1_even)
+        def _():
+            shorter[i].wait_recv()
+
+        @pl.when(jnp.logical_not(c1_even))
+        def _():
+            exchange[i].wait_recv()
+
+
+        if i == FORWARD:
+
+            @pl.when(c0_even)
+            def _():
+                for copy in hops:
+                    copy.wait_send()
+                for copy in forward[: i + 1]:
+                    copy.start()
+
+        if i > FORWARD:
+
+            @pl.when(c0_even)
+            def _():
+                forward[i].start()
+
+        if i == BESIDE:
+
+            @pl.when(c1_odd)
+            def _():
+                hops[0].wait_recv()
+                beside.start()
+
         if i == FIRST:
 
-            @pl.when(helper)
+            @pl.when(c1_odd)
             def _():
-                help_out.wait_recv()
-
-        @pl.when(helper)
-        def _():
-            shorter[i].wait_recv()
-
-        @pl.when(jnp.logical_not(helper))
-        def _():
-            exchange[i].wait_recv()
-
-        @pl.when(helped)
-        def _():
-            forward[i].start()
-
-        @pl.when(helper)
-        def _():
-            for j in LAUNCH[i]:
-                outward[j].start()
+                hops[1].wait_recv()
+                ends[0].start()
+
+        if i == SECOND:
+
+            @pl.when(c0_odd)
+            def _():
+                beside.wait_recv()
+                ends[1].start()
 
     weight.wait_recv()
     wide = wrel[...].astype(F32)
     w3[...] = jnp.concatenate([wide, wide, wide, jnp.zeros_like(wide)], axis=0).astype(BF16)
     codes.wait_recv()
 
-    d_own[...] = jnp.zeros_like(d_own)
-    d_par[...] = jnp.zeros_like(d_par)
-
-    def add(into, held, first_row, first_col, last_col, want, codes_ref):
-        sums = lax.dot_general(
-            held,
-            g2[first_row : first_row + tok, first_col:last_col],
-            (((1,), (1,)), ((), ())),
-            preferred_element_type=F32,
-        )
-        total = jnp.sum(
-            jnp.where(want == codes_ref[0:1, :], sums, 0.0)
-            - jnp.where(want == codes_ref[1:2, :], sums, 0.0),
-            axis=0,
-            keepdims=True,
-        )
-        into[...] += jnp.broadcast_to(total, into.shape)
-
-    def wanted(at, tok_lo):
-        slot = lax.broadcasted_iota(jnp.int32, (span, tok), 0) - tok_lo * caps
-        ours = jnp.logical_and(slot >= 0, slot < caps)
-        return jnp.where(ours, slot + (2 * at + lo) * caps, -2)
-
-    def block(at):
-        here = pl.ds(pl.multiple_of(at * span, 16), span)
-        add(d_own, ebuf[here, :], 0, 0, cols, wanted(at, lo), code_own)
-        theirs = wanted(at, 1 - lo)
-        add(d_par, ebuf[here, cut:], tok, cut, cols, theirs, code_par)
-
-        @pl.when(jnp.logical_not(helper))
-        def _():
-            add(d_par, ebuf[here, :cut], tok, 0, cut, theirs, code_par)
-
-    block(x)
+
+    here = block_rows(x)
+    want = wanted(x)
+    add(tok, 2 * tok, ebuf[here, cut:], cut, cols, want)
+
+    @pl.when(jnp.logical_not(c1_even))
+    def _():
+        add(tok, 2 * tok, ebuf[here, :cut], 0, cut, want)
+
     for k in (0, 2, 1):
 
-        @pl.when(helper)
+        @pl.when(c1_even)
         def _():
             experts_lead[k].wait_recv()
             experts_rest[k].wait_recv()
 
-        @pl.when(jnp.logical_not(helper))
+        @pl.when(jnp.logical_not(c1_even))
         def _():
             experts[k].wait_recv()
 
-        block(lax.rem(x + 3 - k, 4))
-
-    @pl.when(taker)
+        at = lax.rem(x + 3 - k, 4)
+        add_both(block_rows(at), wanted(at))
+
+    @pl.when(c1_odd)
     def _():
         for copy in crossing:
             copy.wait_recv()
+        sums = product(e2[...], 0, tok, 0, cut)
+        slot = lax.broadcasted_iota(jnp.int32, (lead_rows, tok), 0) - (caps - second)
         for at in range(4):
-            slot = lax.broadcasted_iota(jnp.int32, (lead_rows, tok), 0) - (caps - second)
             want = jnp.where(slot >= 0, slot + 2 * at * caps, -2)
-            add(d_own, e2[at * lead_rows : (at + 1) * lead_rows, :], 0, 0, cut, want, code_own)
-
-    back = remote(d_par, d_in, small_send.at[3], small_recv.at[3], partner)
+            pick(0, tok, sums[at * lead_rows : (at + 1) * lead_rows], want)
+
+    back = remote(d_all.at[:, theirs], d_in, small_send.at[3], small_recv.at[3], partner)
     back.start()
-    on = remote(d_par, d_rel_b, small_send.at[4], small_recv.at[4], (before, partner[1]))
+    on = remote(d_all.at[:, theirs], d_rel_b, small_send.at[4], small_recv.at[4], (before, partner[1]))
     on.start()
-    own = remote(d_own, d_rel_a, small_send.at[5], small_recv.at[5], (before, e))
+    own = remote(d_all.at[:, ours], d_rel_a, small_send.at[5], small_recv.at[5], (before, e))
     own.start()
 
     back.wait_recv()
-    rg_ref[...] = coef[...] * (d_own[...] + d_in[...])
+    rg_ref[...] = coef[...] * (d_all[:, ours] + d_in[...])
 
     coefs.wait_recv()
     on.wait_recv()
@@ -366,22 +405,22 @@
     for copy in [weight, codes, coefs, back, on, own]:
         copy.wait_send()
 
-    @pl.when(taker)
+    @pl.when(c1_odd)
     def _():
         for copy in shorter:
             copy.wait_send()
 
-    @pl.when(jnp.logical_not(taker))
+    @pl.when(jnp.logical_not(c1_odd))
     def _():
         for copy in exchange:
             copy.wait_send()
 
-    @pl.when(helper)
+    @pl.when(c1_even)
     def _():
         for copy in experts_lead + experts_rest + crossing:
             copy.wait_send()
 
-    @pl.when(jnp.logical_not(helper))
+    @pl.when(jnp.logical_not(c1_even))
     def _():
         for copy in experts:
             copy.wait_send()
@@ -390,15 +429,19 @@
     def _():
         relay.wait_send()
 
-    @pl.when(helped)
-    def _():
-        for copy in forward + [help_out]:
+    @pl.when(c0_even)
+    def _():
+        for copy in forward:
             copy.wait_send()
 
-    @pl.when(helper)
-    def _():
-        for copy in outward:
-            copy.wait_send()
+    @pl.when(c1_odd)
+    def _():
+        beside.wait_send()
+        ends[0].wait_send()
+
+    @pl.when(c0_odd)
+    def _():
+        ends[1].wait_send()
 
 
 def shards(
@@ -428,12 +471,10 @@
             pltpu.VMEM((experts_n, tok), F32),
             pltpu.VMEM((experts_n, cols), BF16),
             pltpu.VMEM((4 * experts_n, cols), BF16),
-            pltpu.VMEM((2, tok), jnp.int32),
-            pltpu.VMEM((2, tok), jnp.int32),
+            pltpu.VMEM((2, 2 * tok), jnp.int32),
             pltpu.VMEM((experts_n, tok), F32),
             pltpu.VMEM((experts_n, tok), F32),
-            pltpu.VMEM((8, tok), F32),
-            pltpu.VMEM((8, tok), F32),
+            pltpu.VMEM((8, 2 * tok), F32),
             pltpu.VMEM((8, tok), F32),
             pltpu.VMEM((8, tok), F32),
             pltpu.VMEM((8, tok), F32),
@@ -445,9 +486,9 @@
             dma((CHUNKS,)),
             dma((CHUNKS,)),
             dma((CHUNKS + 1,)),
-            dma((CHUNKS,)),
             dma,
-            dma((2,)),
+            dma((5,)),
+            dma((3,)),
             dma((4,)),
             dma((4,)),
             pltpu.SemaphoreType.REGULAR,

time: 49.2 us -> 47.6 us (0.967)
  Pallas kernels: 46.9 us -> 45.3 us
    pallas_call x1, Pallas kernels: 46.9 us -> 45.3 us  [shards(): pl.pallas_call(functools.partial(kernel, caps, lax.axis_size('section')),...]
where the time goes in v3:
time: 47.6 us; the launch traced here: 47.5 us
  Pallas kernels  45.3 us (95%)
  local copies, waits for them, and re-layouts  1.56 us (3%)
  between operations  0.64 us (1%)
    pallas_call x1, Pallas kernels, shards(): pl.pallas_call(functools.partial(kernel, caps, lax.axis_size('section')),...  45.3 us
    unnamed x2, local copies, waits for them, and re-layouts  1.56 us

profile of v3, /device:TPU:1, one launch (start us, length us, event | category | flops | bytes accessed | tf_op | source)
XLA Modules:
  0.0 47.5 jit_solution(14536770703884546805)
XLA Ops:
  0.6 45.3 %combine_router_backward.1 = (bf16[128,4096]{1,0:T(8,128)(2,1)S(1)}, f32[8,128]{1,0:T(8,128)S(1)}) custom-call(bf16[128,4096]{1,0:T(8,128)(2,1)} %bitcast.24, bf16[320,4096]{1,0:T(8,128)(2,1)} %bitcast.23, s32[2,128]{1,0:T(2,128)} %bitcast.27, s32[2,128]{1,0:T(2,128)} %bitcast.28, s32[2,128]{1,0:T(2,128)} %bitcast.29, f32[8,128]{1,0:T(8,128)} %bitcast.26, ...), custom_call_target="tpu_custom_call" | custom-call | flops 700000000 | bytes 8000000 | tf_op jit(solution)/shard_map/combine_router_backward/pallas_call | solution.py:454
  46.0 1.0 %copy.11 = bf16[1,128,4096]{2,1,0:T(8,128)(2,1)} copy(bf16[1,128,4096]{2,1,0:T(8,128)(2,1)S(1)} %bitcast.21) | data formatting | bytes 2097152
  46.9 0.6 %copy.12 = f32[1,128,8]{1,2,0:T(8,128)} copy(f32[1,128,8]{1,2,0:T(8,128)S(1)} %bitcast.22) | data formatting | bytes 8192

commit v4 on v3

--- a/solution.py
+++ b/solution.py
@@ -14,6 +14,7 @@
 FIRST = 5
 SECOND = 5
 SHARE = 1
+PIECES = 4
 F32 = jnp.float32
 BF16 = jnp.bfloat16
 
@@ -28,11 +29,12 @@
     keep_hbm,
     logits_hbm,
     w_hbm,
-    out_ref,
+    grel,
+    w3,
+    grad_ref,
     rg_ref,
     g2,
     ebuf,
-    grel,
     hbuf,
     e2,
     ids,
@@ -40,7 +42,6 @@
     keep,
     logits,
     wrel,
-    w3,
     code_all,
     coef,
     coef_rel,
@@ -389,59 +390,72 @@
     coefs.wait_recv()
     on.wait_recv()
     own.wait_recv()
-    grad = coef_rel[...] * (d_rel_a[...] + d_rel_b[...])
+    grad_ref[...] = coef_rel[...] * (d_rel_a[...] + d_rel_b[...])
+    relay.wait_recv()
+
+    for copy in [weight, codes, coefs, back, on, own]:
+        copy.wait_send()
+
+    @pl.when(c1_odd)
+    def _():
+        for copy in shorter:
+            copy.wait_send()
+
+    @pl.when(jnp.logical_not(c1_odd))
+    def _():
+        for copy in exchange:
+            copy.wait_send()
+
+    @pl.when(c1_even)
+    def _():
+        for copy in experts_lead + experts_rest + crossing:
+            copy.wait_send()
+
+    @pl.when(jnp.logical_not(c1_even))
+    def _():
+        for copy in experts:
+            copy.wait_send()
+
+    @pl.when(inside)
+    def _():
+        relay.wait_send()
+
+    @pl.when(c0_even)
+    def _():
+        for copy in forward:
+            copy.wait_send()
+
+    @pl.when(c1_odd)
+    def _():
+        beside.wait_send()
+        ends[0].wait_send()
+
+    @pl.when(c0_odd)
+    def _():
+        ends[1].wait_send()
+
+
+def finish(rows_ref, w3, grad_ref, rg_ref, out_hbm, rg_hbm, out_ref, sem):
+    cols = rows_ref.shape[1]
+    rg_copy = pltpu.make_async_copy(rg_ref, rg_hbm, sem.at[PIECES])
+    rg_copy.start()
+    grad = grad_ref[...]
     high = grad.astype(BF16)
     rest = grad - high.astype(F32)
     mid = rest.astype(BF16)
     low = rest - mid.astype(F32)
     pieces = jnp.concatenate([high.astype(F32), mid.astype(F32), low, jnp.zeros_like(low)], axis=0)
     left = pieces.T.astype(BF16)
-    relay.wait_recv()
-    step = 512
-    for at in range(0, cols, step):
-        term = jnp.dot(left, w3[:, at : at + step], preferred_element_type=F32)
-        out_ref[:, at : at + step] = (grel[:, at : at + step].astype(F32) + term).astype(BF16)
-
-    for copy in [weight, codes, coefs, back, on, own]:
-        copy.wait_send()
-
-    @pl.when(c1_odd)
-    def _():
-        for copy in shorter:
-            copy.wait_send()
-
-    @pl.when(jnp.logical_not(c1_odd))
-    def _():
-        for copy in exchange:
-            copy.wait_send()
-
-    @pl.when(c1_even)
-    def _():
-        for copy in experts_lead + experts_rest + crossing:
-            copy.wait_send()
-
-    @pl.when(jnp.logical_not(c1_even))
-    def _():
-        for copy in experts:
-            copy.wait_send()
-
-    @pl.when(inside)
-    def _():
-        relay.wait_send()
-
-    @pl.when(c0_even)
-    def _():
-        for copy in forward:
-            copy.wait_send()
-
-    @pl.when(c1_odd)
-    def _():
-        beside.wait_send()
-        ends[0].wait_send()
-
-    @pl.when(c0_odd)
-    def _():
-        ends[1].wait_send()
+    step = cols // PIECES
+    copies = []
+    for k in range(PIECES):
+        at = pl.ds(k * step, step)
+        term = jnp.dot(left, w3[:, at], preferred_element_type=F32)
+        out_ref[:, at] = (rows_ref[:, at].astype(F32) + term).astype(BF16)
+        copies.append(pltpu.make_async_copy(out_ref.at[:, at], out_hbm.at[:, at], sem.at[k]))
+        copies[-1].start()
+    for copy in copies + [rg_copy]:
+        copy.wait()
 
 
 def shards(
@@ -451,18 +465,19 @@
     experts_n = router_logits.shape[2]
     caps = expert_outputs.shape[1] // experts_n
     dma = pltpu.SemaphoreType.DMA
-    passed, grad = pl.pallas_call(
+    rows, w3, grad_next, grad_own = pl.pallas_call(
         functools.partial(kernel, caps, lax.axis_size("section")),
         out_shape=(
             jax.ShapeDtypeStruct((tok, cols), BF16),
+            jax.ShapeDtypeStruct((4 * experts_n, cols), BF16),
+            jax.ShapeDtypeStruct((experts_n, tok), F32),
             jax.ShapeDtypeStruct((experts_n, tok), F32),
         ),
         in_specs=[pl.BlockSpec(memory_space=pltpu.HBM)] * 7,
-        out_specs=(pl.BlockSpec(memory_space=pltpu.VMEM), pl.BlockSpec(memory_space=pltpu.VMEM)),
+        out_specs=(pl.BlockSpec(memory_space=pltpu.VMEM),) * 4,
         scratch_shapes=[
             pltpu.VMEM((2 * tok, cols), BF16),
             pltpu.VMEM((8 * caps, cols), BF16),
-            pltpu.VMEM((tok, cols), BF16),
             pltpu.VMEM((tok, cols), BF16),
             pltpu.VMEM((4 * (caps // 16 * 16 + 16), cols // 8 * SHARE), BF16),
             pltpu.VMEM((2, tok), jnp.int32),
@@ -470,7 +485,6 @@
             pltpu.VMEM((2, tok), jnp.int32),
             pltpu.VMEM((experts_n, tok), F32),
             pltpu.VMEM((experts_n, cols), BF16),
-            pltpu.VMEM((4 * experts_n, cols), BF16),
             pltpu.VMEM((2, 2 * tok), jnp.int32),
             pltpu.VMEM((experts_n, tok), F32),
             pltpu.VMEM((experts_n, tok), F32),
@@ -512,6 +526,18 @@
             )
         )
     )
+    passed, grad = pl.pallas_call(
+        finish,
+        out_shape=(
+            jax.ShapeDtypeStruct((tok, cols), BF16),
+            jax.ShapeDtypeStruct((experts_n, tok), F32),
+        ),
+        in_specs=[pl.BlockSpec(memory_space=pltpu.VMEM)] * 4,
+        out_specs=(pl.BlockSpec(memory_space=pltpu.HBM),) * 2,
+        scratch_shapes=[pltpu.VMEM((tok, cols), BF16), pltpu.SemaphoreType.DMA((PIECES + 1,))],
+        compiler_params=pltpu.CompilerParams(vmem_limit_bytes=16 << 20),
+        name="router_term",
+    )(rows, w3, grad_next, grad_own)
     return (passed[None], grad.T[None])
 
 

time: 47.6 us -> 47 us (0.987)
  local copies, waits for them, and re-layouts: 1.56 us -> 0 us
  Pallas kernels: 45.3 us -> 46.2 us
    unnamed x2 -> x0, local copies, waits for them, and re-layouts: 1.56 us -> none
    pallas_call x0 -> x1, Pallas kernels: none -> 1.28 us  [shards(): pl.pallas_call(finish, out_shape=(jax.ShapeDtypeStruct((tok, cols), BF16)...]
where the time goes in v4:
time: 47 us; the launch traced here: 46.8 us
  Pallas kernels  46.2 us (98%)
  between operations  0.64 us (1%)
    pallas_call x1, Pallas kernels, shards(): pl.pallas_call(functools.partial(kernel, caps, lax.axis_size('section')),...  44.9 us
    pallas_call x1, Pallas kernels, shards(): pl.pallas_call(finish, out_shape=(jax.ShapeDtypeStruct((tok, cols), BF16)...  1.28 us

profile of v4, /device:TPU:1, one launch (start us, length us, event | category | flops | bytes accessed | tf_op | source)
XLA Modules:
  0.0 46.8 jit_solution(13890293944666701369)
XLA Ops:
  0.6 44.9 %combine_router_backward.1 = (bf16[128,4096]{1,0:T(8,128)(2,1)S(1)}, bf16[32,4096]{1,0:T(8,128)(2,1)S(1)}, f32[8,128]{1,0:T(8,128)S(1)}, f32[8,128]{1,0:T(8,128)S(1)}) custom-call(bf16[128,4096]{1,0:T(8,128)(2,1)} %bitcast.22, bf16[320,4096]{1,0:T(8,128)(2,1)} %bitcast.21, s32[2,128]{1,0:T(2,128)} %bitcast.25, s32[2,128]{1,0:T(2,128)} %bitcast.26, ...), custom_call_target="tpu_custom_call" | custom-call | flops 700000000 | bytes 8000000 | tf_op jit(solution)/shard_map/combine_router_backward/pallas_call | solution.py:468
  45.5 1.3 %router_term.1 = (bf16[128,4096]{1,0:T(8,128)(2,1)}, f32[8,128]{1,0:T(8,128)}) custom-call(bf16[128,4096]{1,0:T(8,128)(2,1)S(1)} %get-tuple-element.8.rows_ref, bf16[32,4096]{1,0:T(8,128)(2,1)S(1)} %get-tuple-element.9.w3, f32[8,128]{1,0:T(8,128)S(1)} %get-tuple-element.10.grad_ref, f32[8,128]{1,0:T(8,128)S(1)} %get-tuple-element.11.rg_ref), custom_call_target="tpu_custom_call" | custom-call | tf_op jit(solution)/shard_map/router_term/pallas_call | solution.py:529

commit v5 on v4

--- a/solution.py
+++ b/solution.py
@@ -9,6 +9,7 @@
 
 MESH = pl.DeviceIdType.MESH
 CHUNKS = 8
+ASIDE = 4
 FORWARD = 4
 BESIDE = 3
 FIRST = 5
@@ -217,10 +218,6 @@
         for copy in hops:
             copy.start()
 
-    @pl.when(inside)
-    def _():
-        relay.start()
-
     weight = remote(w_hbm, wrel, small_send.at[0], small_recv.at[0], (before, e))
     weight.start()
 
@@ -317,6 +314,12 @@
             @pl.when(c0_even)
             def _():
                 forward[i].start()
+
+        if i == ASIDE:
+
+            @pl.when(inside)
+            def _():
+                relay.start()
 
         if i == BESIDE:
 

time: 47 us -> 47 us (level)
  no operation moved by 1% of the time
where the time goes in v5:
time: 47 us; the launch traced here: 46.8 us
  Pallas kernels  46.2 us (98%)
  between operations  0.64 us (1%)
    pallas_call x1, Pallas kernels, shards(): pl.pallas_call(functools.partial(kernel, caps, lax.axis_size('section')),...  44.9 us
    pallas_call x1, Pallas kernels, shards(): pl.pallas_call(finish, out_shape=(jax.ShapeDtypeStruct((tok, cols), BF16)...  1.28 us

profile of v5, /device:TPU:1, one launch (start us, length us, event | category | flops | bytes accessed | tf_op | source)
XLA Modules:
  0.0 46.8 jit_solution(9791814120743380930)
XLA Ops:
  0.6 44.9 %combine_router_backward.1 = (bf16[128,4096]{1,0:T(8,128)(2,1)S(1)}, bf16[32,4096]{1,0:T(8,128)(2,1)S(1)}, f32[8,128]{1,0:T(8,128)S(1)}, f32[8,128]{1,0:T(8,128)S(1)}) custom-call(bf16[128,4096]{1,0:T(8,128)(2,1)} %bitcast.22, bf16[320,4096]{1,0:T(8,128)(2,1)} %bitcast.21, s32[2,128]{1,0:T(2,128)} %bitcast.25, s32[2,128]{1,0:T(2,128)} %bitcast.26, ...), custom_call_target="tpu_custom_call" | custom-call | flops 700000000 | bytes 8000000 | tf_op jit(solution)/shard_map/combine_router_backward/pallas_call | solution.py:471
  45.5 1.3 %router_term.1 = (bf16[128,4096]{1,0:T(8,128)(2,1)}, f32[8,128]{1,0:T(8,128)}) custom-call(bf16[128,4096]{1,0:T(8,128)(2,1)S(1)} %get-tuple-element.8.rows_ref, bf16[32,4096]{1,0:T(8,128)(2,1)S(1)} %get-tuple-element.9.w3, f32[8,128]{1,0:T(8,128)S(1)} %get-tuple-element.10.grad_ref, f32[8,128]{1,0:T(8,128)S(1)} %get-tuple-element.11.rg_ref), custom_call_target="tpu_custom_call" | custom-call | tf_op jit(solution)/shard_map/router_term/pallas_call | solution.py:532
